TPU v7x, 256 devices: a whole 4x4x8 slice. The times are simulated.
256 devices in a mesh: seq: 8 (over z), exp: 32 (over x, y, core).
Axes of the slice: x: 4, y: 4, z: 8, core: 2. Of those that a mesh axis runs over, the one named last changes fastest.
Arguments:
- tokens: bfloat16 [32, 512, 4096], P('exp', 'seq'), may hold values from -6 to 6
- queries: bfloat16 [32, 512, 4096], P('exp', 'seq'), may hold values from -6 to 6
- memory_kv: bfloat16 [512, 1024], P('exp'), may hold values from -6 to 6
- memory_pos: int32 [512], P('exp'), may hold values from 0 to 1023
- out_weight: bfloat16 [4096, 4096], P('seq'), may hold values from -1.5 to 1.5
- norm_gain: float32 [4096], replicated, may hold values from 0.5 to 1.5
- routes: int32 [32, 512, 2], P('exp', 'seq'), may hold values from 0 to 31, all different within a row; in each aligned block of 64 rows (0 to 63, 64 to 127, ..., all dimensions but the last counted through in order) at most 5 rows name the same one
- route_weights: float32 [32, 512, 2], P('exp', 'seq'), may hold values from 0.05 to 1
- gate_w: bfloat16 [32, 4096, 1536], P('exp', None, 'seq'), may hold values from -0.09375 to 0.09375
- up_w: bfloat16 [32, 4096, 1536], P('exp', None, 'seq'), may hold values from -0.09375 to 0.09375
- down_w: bfloat16 [32, 1536, 4096], P('exp', 'seq'), may hold values from -0.15625 to 0.15625
Outputs:
- attended: bfloat16 [32, 512, 4096], P('exp', 'seq')
- mixture: bfloat16 [32, 512, 4096], P('exp', 'seq')
Inputs may be any that keep to these rules, and one draw needn't show every extreme that they name: `routes`: each token names 2 different experts. Taking the tokens in order of span and then place, among each aligned block of 64 tokens (the tokens of one device) no expert is named more than 5 times, and in every draw some expert is named exactly 5 times within one block.
All inputs are finite; a program needn't handle non-finite values.
Results may differ from a plain program's by a relative error of at most 0.035.
Values may be sent and summed in bfloat16 or wider, within the bound.
A program may use at most 128 MiB of HBM per device.

v0:
```python
import math

import jax
import jax.numpy as jnp
from jax import lax
from jax.sharding import PartitionSpec as P

KVH = 4
EXPERTS = 32
TOPK = 2
CAP = 5


def attend(query_rows, memory_rows, allowed, kv_heads):
    row_count = query_rows.shape[0]
    head_width = memory_rows.shape[1] // (2 * kv_heads)
    query_heads = query_rows.shape[1] // head_width
    grouped = query_rows.reshape(row_count, kv_heads, query_heads // kv_heads, head_width)
    paired = memory_rows.reshape(memory_rows.shape[0], kv_heads, 2, head_width)
    key_rows = paired[:, :, 0, :]
    value_rows = paired[:, :, 1, :]
    scores = jnp.einsum("rgcd,mgd->gcrm", grouped, key_rows, preferred_element_type=jnp.float32) * (
        1.0 / math.sqrt(head_width)
    )
    scores = jnp.where(allowed[None, None], scores, -1e30)
    top_score = jnp.max(scores, axis=3, keepdims=True)
    weights = jnp.exp(scores - top_score)
    probabilities = (weights / jnp.sum(weights, axis=3, keepdims=True)).astype(jnp.bfloat16)
    context = jnp.einsum(
        "gcrm,mgd->rgcd", probabilities, value_rows, preferred_element_type=jnp.float32
    ).astype(jnp.bfloat16)
    return context.reshape(row_count, query_heads * head_width)


def body(
    tokens,
    queries,
    memory_kv,
    memory_pos,
    out_weight,
    norm_gain,
    routes,
    route_weights,
    gate_w,
    up_w,
    down_w,
):
    seq_count = lax.axis_size("seq")
    seq_index = lax.axis_index("seq")
    tok_rows = tokens.shape[1]
    width = tokens.shape[2]
    span_len = tok_rows * seq_count
    own_tokens = tokens.reshape(tok_rows, width)
    own_queries = queries.reshape(tok_rows, queries.shape[2])
    places = lax.all_gather(memory_pos, "exp", axis=0, tiled=True)
    memory_rows = lax.all_gather(memory_kv, "exp", axis=0, tiled=True)
    positions = span_len + seq_index * tok_rows + jnp.arange(tok_rows, dtype=jnp.int32)
    allowed = places[None, :] <= positions[:, None]
    own_context = attend(own_queries, memory_rows, allowed, KVH)
    context = lax.all_to_all(own_context, "seq", split_axis=1, concat_axis=0, tiled=True)
    rows_part = context
    projected = lax.psum_scatter(
        jnp.dot(rows_part, out_weight, preferred_element_type=jnp.float32).astype(jnp.bfloat16),
        "seq",
        scatter_dimension=0,
        tiled=True,
    ).astype(jnp.float32)
    attended = projected.astype(jnp.bfloat16)
    summed = own_tokens.astype(jnp.float32) + projected
    normed = (
        summed * lax.rsqrt(jnp.mean(summed * summed, axis=1, keepdims=True) + 1e-06) * norm_gain
    ).astype(jnp.bfloat16)
    flat_routes = routes.reshape(-1)
    expert_ids = jnp.arange(EXPERTS, dtype=jnp.int32)
    one_hot = (flat_routes[:, None] == expert_ids[None, :]).astype(jnp.int32)
    slot_index = jnp.sum((jnp.cumsum(one_hot, axis=0) - 1) * one_hot, axis=1)
    send_index = flat_routes * CAP + slot_index
    slot_ids = jnp.arange(EXPERTS * CAP, dtype=jnp.int32)
    pick_rows = (send_index[None, :] == slot_ids[:, None]).reshape(EXPERTS * CAP, tok_rows, TOPK)
    pick_rows = jnp.any(pick_rows, axis=2).astype(jnp.bfloat16)
    outgoing = jnp.dot(pick_rows, normed, preferred_element_type=jnp.float32).astype(jnp.bfloat16)
    outgoing = outgoing.reshape(EXPERTS, CAP, width)
    incoming = lax.all_to_all(outgoing, "exp", split_axis=0, concat_axis=1, tiled=True)
    rows_piece = lax.all_gather(incoming, "seq", axis=1, tiled=True)
    gate_act = jnp.einsum("enk,ekf->enf", rows_piece, gate_w, preferred_element_type=jnp.float32)
    up_act = jnp.einsum("enk,ekf->enf", rows_piece, up_w, preferred_element_type=jnp.float32)
    hidden = (jax.nn.silu(gate_act) * up_act).astype(jnp.bfloat16)
    hidden_all = jnp.transpose(hidden, (1, 0, 2))
    rows_part = hidden_all
    returned = lax.psum_scatter(
        jnp.einsum("nef,efk->nek", rows_part, down_w, preferred_element_type=jnp.float32).astype(
            jnp.bfloat16
        ),
        "seq",
        scatter_dimension=0,
        tiled=True,
    )
    returned_rows = lax.all_to_all(returned, "exp", split_axis=0, concat_axis=1, tiled=True)
    back_index = slot_index * EXPERTS + flat_routes
    weight_matrix = (back_index[None, :] == slot_ids[:, None]).astype(
        jnp.float32
    ) * route_weights.reshape(-1)[None, :]
    weight_matrix = jnp.sum(weight_matrix.reshape(EXPERTS * CAP, tok_rows, TOPK), axis=2)
    gathered_out = returned_rows.reshape(CAP * EXPERTS, width).astype(jnp.float32)
    mixture = jnp.dot(weight_matrix.T, gathered_out, precision=lax.Precision.HIGHEST)
    return (
        attended.reshape(1, tok_rows, width),
        mixture.astype(jnp.bfloat16).reshape(1, tok_rows, width),
    )


def solution(mesh):
    in_specs = (
        P("exp", "seq", None),
        P("exp", "seq", None),
        P("exp", None),
        P("exp"),
        P("seq", None),
        P(),
        P("exp", "seq", None),
        P("exp", "seq", None),
        P("exp", None, "seq"),
        P("exp", None, "seq"),
        P("exp", "seq", None),
    )
    out_specs = (P("exp", "seq", None), P("exp", "seq", None))
    return jax.shard_map(body, mesh=mesh, in_specs=in_specs, out_specs=out_specs, check_vma=False)
```

profile of v0, /device:TPU:1, one launch (start us, length us, event | category | flops | bytes accessed | tf_op | source)
XLA Modules:
  0.0 499.7 jit_solution(13594640370777830428)
XLA Ops:
  7.2 0.0 copy-start
  7.2 0.0 all-gather.3.cloned.1.call-start
  7.2 0.7 all-gather.3.cloned.1.call-update
  7.9 0.0 reduce-scatter.3.cloned.1.call-start
  8.0 1.1 copy.70
  9.1 1.3 dynamic-slice
  11.0 0.9 dynamic-update-slice
  11.9 14.4 %all-reduce = s32[512]{0:T(512)S(1)} all-reduce(s32[512]{0:T(512)S(1)} %dynamic-update-slice), channel_id=1, replica_groups=mesh['seq'=8,'exp'=32] {'exp'}, use_global_device_ids=true, to_apply=%add | all-reduce | flops 512 | bytes 4096
  26.4 0.1 broadcast_compare_fusion
  26.5 36.2 %all-gather.3.cloned.1.call-done = bf16[512,1024]{1,0:T(8,128)(2,1)} async-done(((bf16[16,1024]{1,0:T(8,128)(2,1)}), bf16[512,1024]{1,0:T(8,128)(2,1)}) %all-gather.3.cloned.1.call-update) | async-done | bytes 1048592 | tf_op jit(solution)/shard_map/all_gather | solution.py:56
  62.7 1.5 copy.54
  64.2 0.7 fusion.32
  64.9 1.7 fusion.44
  66.6 0.8 fusion.26
  67.3 0.3 copy.58
  67.7 0.3 all_to_all.34
  68.0 0.2 copy.59
  68.2 24.2 %all_to_all.46 = bf16[64,8,512]{2,0,1:T(8,128)(2,1)S(1)} all-to-all(bf16[64,8,512]{2,0,1:T(8,128)(2,1)S(1)} %copy.59), channel_id=1, replica_groups=mesh['seq'=8,'exp'=32] {'seq'}, dimensions={1} | all-to-all | bytes 1048576 | tf_op jit(solution)/shard_map/all_to_all | solution.py:60
  92.3 6.5 %convolution_convert_fusion.1 = bf16[512,4096]{1,0:T(8,128)(2,1)} fusion(bf16[512,512]{1,0:T(8,128)(2,1)S(1)} %bitcast.96, bf16[512,4096]{1,0:T(8,128)(2,1)} %param.15), kind=kOutput, calls=%fused_computation.7 | convolution fusion | flops 2149580800 | bytes 8912896 | tf_op jit(solution)/shard_map/dot_general | solution.py:63
  98.8 0.0 copy-start.3
  98.8 0.0 copy-start.1
  98.8 0.0 copy-start.2
  98.8 0.0 reduce-scatter.3.cloned.1.call-update
  98.8 0.0 all-gather.5.cloned.1.call-start
  98.9 0.6 copy-done.3
  99.5 0.1 copy.60
  99.6 0.1 eq.43
  99.7 0.1 fusion.39
  99.8 0.2 reduce_window_sum.11
  100.0 0.2 select_reduce_fusion.1
  100.2 0.1 reduce_sum.40
  100.3 0.1 copy.61
  100.4 0.1 fusion.38
  100.5 48.2 %reduce-scatter.3.cloned.1.call-done = bf16[64,4096]{1,0:T(8,128)(2,1)} async-done(((bf16[512,4096]{1,0:T(8,128)(2,1)}), bf16[64,4096]{1,0:T(8,128)(2,1)}) %reduce-scatter.3.cloned.1.call-update) | async-done | bytes 524304 | tf_op jit(solution)/shard_map/reduce_scatter | solution.py:62
  148.7 0.0 copy-done.1
  148.7 1.3 multiply_reduce_fusion
  150.0 0.0 copy-done.2
  150.0 1.6 convolution_convert_fusion.2
  151.7 1.6 reshape.150
  153.2 0.0 copy-start.5
  153.2 35.9 %all_to_all.47 = bf16[32,5,4096]{2,1,0:T(8,128)(2,1)} all-to-all(bf16[32,5,4096]{2,1,0:T(8,128)(2,1)} %reshape.150), channel_id=1, replica_groups=mesh['seq'=8,'exp'=32] {'exp'}, dimensions={0} | all-to-all | bytes 2621440 | tf_op jit(solution)/shard_map/all_to_all | solution.py:83
  189.1 2.7 all_to_all.39
  191.8 0.0 all-gather.5.cloned.1.call-update
  191.8 0.2 reduce-scatter.5.cloned.1.call-start
  192.0 108.8 %all-gather.5.cloned.1.call-done = bf16[1,1280,4096]{2,1,0:T(8,128)(2,1)} async-done(((bf16[1,160,4096]{2,1,0:T(8,128)(2,1)}), bf16[1,1280,4096]{2,1,0:T(8,128)(2,1)}) %all-gather.5.cloned.1.call-update) | async-done | bytes 10485776 | tf_op jit(solution)/shard_map/all_gather | solution.py:84
  300.8 0.0 copy-done.5
  300.8 8.5 %fusion.4 = f32[1280,192]{0,1:T(8,128)} fusion(bf16[1,1280,4096]{2,1,0:T(8,128)(2,1)} %all-gather.5.cloned.1.call-done, bf16[1,4096,192]{1,2,0:T(8,128)(2,1)S(1)} %copy-done.5), kind=kOutput, calls=%fused_computation.5 | convolution fusion | flops 2013265920 | bytes 13041664 | tf_op jit(solution)/shard_map/enk,ekf->enf/dot_general | solution.py:85
  309.3 0.0 copy-done
  309.3 19.0 %fusion.1 = bf16[1280,1,4096]{2,0,1:T(8,128)(2,1)} fusion(bf16[1,192,4096]{2,1,0:T(8,128)(2,1)S(1)} %copy-done, bf16[1,1280,4096]{2,1,0:T(8,128)(2,1)} %all-gather.5.cloned.1.call-done, bf16[1,4096,192]{1,2,0:T(8,128)(2,1)} %param.20, f32[1280,192]{0,1:T(8,128)} %fusion.4), kind=kOutput, calls=%fused_computation.2 | convolution fusion | flops 4033249280 | bytes 25100288 | tf_op jit(solution)/shard_map/nef,efk->nek/dot_general | solution.py:91
  328.3 0.0 reduce-scatter.5.cloned.1.call-update
  328.4 0.0 copy-start.4
  328.4 113.5 %reduce-scatter.5.cloned.1.call-done = bf16[160,1,4096]{2,0,1:T(8,128)(2,1)} async-done(((bf16[1280,1,4096]{2,0,1:T(8,128)(2,1)}), bf16[160,1,4096]{2,0,1:T(8,128)(2,1)}) %reduce-scatter.5.cloned.1.call-update) | async-done | bytes 1310736 | tf_op jit(solution)/shard_map/reduce_scatter | solution.py:90
  441.9 0.5 broadcast.81
  442.4 2.9 reduce.1
  445.3 1.9 reshape.166
  447.2 7.5 %all-to-all-start.2 = ((bf16[32,2,10240]{2,1,0:T(2,128)(2,1)}), bf16[32,2,10240]{2,1,0:T(2,128)(2,1)S(1)}, u32[]{:S(2)}, u32[]{:S(2)}) async-start(bf16[32,2,10240]{2,1,0:T(2,128)(2,1)} %reshape.166), calls=%async_computation.4 | async-start | bytes 2621440 | tf_op jit(solution)/shard_map/all_to_all | solution.py:98
  454.8 0.0 copy-done.4
  454.8 0.1 select_reduce_fusion
  454.9 19.7 %all-to-all-done.2 = bf16[32,2,10240]{2,1,0:T(2,128)(2,1)S(1)} async-done(((bf16[32,2,10240]{2,1,0:T(2,128)(2,1)}), bf16[32,2,10240]{2,1,0:T(2,128)(2,1)S(1)}, u32[]{:S(2)}, u32[]{:S(2)}) %all-to-all-start.2) | async-done | bytes 1310752 | tf_op jit(solution)/shard_map/all_to_all | solution.py:98
  474.5 3.7 reshape.167
  478.2 9.4 %reduce = bf16[160,4096]{1,0:T(8,128)(2,1)S(1)} reduce(bf16[160,1,4096]{2,1,0:T(2,128)(2,1)} %reshape.167, bf16[]{:T(256)} %constant.57), dimensions={1}, to_apply=%all_to_all.40.reduce_sub_computation | reduce | bytes 2621442 | tf_op jit(solution)/shard_map/all_to_all | solution.py:98
  487.6 1.6 all_to_all.41
  489.3 2.5 copy.64
  491.7 1.5 fusion.6
  (4 shorter events, 0.0 us)
Async XLA Ops:
  7.2 302.1 %copy-start = (bf16[1,192,4096]{2,1,0:T(8,128)(2,1)S(1)}, bf16[1,192,4096]{2,1,0:T(8,128)(2,1)}, u32[]{:S(2)}) copy-start(bf16[1,192,4096]{2,1,0:T(8,128)(2,1)} %param.21) | copy-start | bytes 4718596
  7.2 55.5 %all-gather.3.cloned.1.call-start = ((), (), s32[]{:S(2)}) async-start(), calls=%async_computation.5 | async-start | bytes 1081344 | tf_op jit(solution)/shard_map/all_gather | solution.py:56
  7.9 140.8 %reduce-scatter.3.cloned.1.call-start = ((), (), s32[]{:S(2)}) async-start(), calls=%async_computation.6 | async-start | bytes 4718592 | tf_op jit(solution)/shard_map/reduce_scatter | solution.py:62
  98.8 0.7 copy-start.3
  98.8 49.9 %copy-start.1 = (bf16[1,64,4096]{2,1,0:T(8,128)(2,1)S(1)}, bf16[1,64,4096]{2,1,0:T(8,128)(2,1)}, u32[]{:S(2)}) copy-start(bf16[1,64,4096]{2,1,0:T(8,128)(2,1)} %param.11) | copy-start | bytes 1572868
  98.8 51.2 %copy-start.2 = (f32[4096]{0:T(1024)S(1)}, f32[4096]{0:T(1024)}, u32[]{:S(2)}) copy-start(f32[4096]{0:T(1024)} %param.16) | copy-start | bytes 49156
  98.8 202.0 %all-gather.5.cloned.1.call-start = ((), (), s32[]{:S(2)}) async-start(), calls=%async_computation.7 | async-start | bytes 11796480 | tf_op jit(solution)/shard_map/all_gather | solution.py:84
  153.2 147.6 %copy-start.5 = (bf16[1,4096,192]{1,2,0:T(8,128)(2,1)S(1)}, bf16[1,4096,192]{1,2,0:T(8,128)(2,1)}, u32[]{:S(2)}) copy-start(bf16[1,4096,192]{1,2,0:T(8,128)(2,1)} %param.19) | copy-start | bytes 4718596
  191.8 250.1 %reduce-scatter.5.cloned.1.call-start = ((), (), s32[]{:S(2)}) async-start(), calls=%async_computation.8 | async-start | bytes 11796480 | tf_op jit(solution)/shard_map/reduce_scatter | solution.py:90
  328.4 126.4 %copy-start.4 = (f32[1,64,2]{1,2,0:T(2,128)S(1)}, f32[1,64,2]{1,2,0:T(2,128)}, u32[]{:S(2)}) copy-start(f32[1,64,2]{1,2,0:T(2,128)} %param.18) | copy-start | bytes 1540
  447.2 27.3 %all-to-all-start.2 = ((bf16[32,2,10240]{2,1,0:T(2,128)(2,1)}), bf16[32,2,10240]{2,1,0:T(2,128)(2,1)S(1)}, u32[]{:S(2)}, u32[]{:S(2)}) async-start(bf16[32,2,10240]{2,1,0:T(2,128)(2,1)} %reshape.166), calls=%async_computation.4 | async-start | bytes 2621440 | tf_op jit(solution)/shard_map/all_to_all | solution.py:98
Sparse Core Ops, SparseCore 0:
  10.6 52.0 all-gather.2
  99.0 49.6 reduce-scatter.2
  191.9 108.8 all-gather.4
  328.5 113.3 reduce-scatter.4
where the time goes:
time: 500 us
  waiting for transfers between devices  327 us (65%)
  blocking collectives  74.5 us (15%)
  matrix products  38.5 us (8%)
  local copies, waits for them, and re-layouts  21.1 us (4%)
  other arithmetic  16.1 us (3%)
  between operations  14.6 us (3%)
  starting transfers between devices  7.85 us (2%)
    reduce_scatter x1, waiting for transfers between devices, body(): lax.psum_scatter(jnp.einsum('nef,efk->nek', rows_part, down_w, preferred_...  113 us
    all_gather x1, waiting for transfers between devices, body(): rows_piece = lax.all_gather(incoming, 'seq', axis=1, tiled=True)  109 us
    reduce_scatter x1, waiting for transfers between devices, body(): lax.psum_scatter(jnp.dot(rows_part, out_weight, preferred_element_type=jn...  48.2 us
    all_gather x1, waiting for transfers between devices, body(): memory_rows = lax.all_gather(memory_kv, 'exp', axis=0, tiled=True)  36.2 us
    all_to_all x1, blocking collectives, body(): lax.all_to_all(outgoing, 'exp', split_axis=0, concat_axis=1, tiled=True)  35.9 us
    all_to_all x1, blocking collectives, body(): lax.all_to_all(own_context, 'seq', split_axis=1, concat_axis=0, tiled=True)  24.2 us
    all_to_all x1, waiting for transfers between devices, body(): lax.all_to_all(returned, 'exp', split_axis=0, concat_axis=1, tiled=True)  19.7 us
    dot_general x1, matrix products, body(): jnp.einsum('nef,efk->nek', rows_part, down_w, preferred_element_type=jnp....  19 us
  transfers between devices with their start and end apart: 5, of which 5 were waited for; matrix products, arithmetic and copies ran while one was open for 1% of the time, Pallas kernels for 0%

commit v1 on v0

v1 whole, which is shorter than its diff:
```python
import functools
import math

import jax
import jax.numpy as jnp
from jax import lax
from jax.experimental import pallas as pl
from jax.experimental.pallas import tpu as pltpu
from jax.sharding import PartitionSpec as P

MESH = pl.DeviceIdType.MESH
EXPERTS = 32
CAP = 5
RING = 8
D = 4096
HALF = D // 2
HD = 128
TOK = 64
MEM = 512
KEYS = 512
UNITS = 192
SLOTS = EXPERTS * CAP
LANES = HALF // 128
PIECE = LANES * CAP
F32 = jnp.float32
BF16 = jnp.bfloat16

HOPS = [
    (dx, dy, dc)
    for dc in range(2)
    for dx, dy in [
        (2, 2), (1, 1), (3, 3), (2, 1), (1, 2), (2, 3), (3, 2), (1, 3),
        (3, 1), (2, 0), (0, 2), (1, 0), (3, 0), (0, 1), (0, 3), (0, 0),
    ]
    if (dx, dy, dc) != (0, 0, 0)
]


def exp_peers(e):
    x, y, c = e // 8, (e // 2) % 4, e % 2
    return [((x + dx) % 4 * 8) + ((y + dy) % 4 * 2) + (c + dc) % 2 for dx, dy, dc in HOPS]


def cols(half):
    return pl.ds(half * HALF, HALF)


def ring_send(src, dst, sems, way, step, half, z, e):
    target = ((z + (1 if way == 0 else RING - 1)) % RING, e)
    copy = pltpu.make_async_remote_copy(
        src_ref=src,
        dst_ref=dst,
        send_sem=sems[0].at[way, step, half],
        recv_sem=sems[1].at[way, step, half],
        device_id=target,
        device_id_type=MESH,
    )
    copy.start()
    return copy


def reduce_ring(stage, land, sems, z, e, sent, compute, early):
    def push(way, step, half):
        k = (4 - step) if way == 0 else (4 + step) % RING
        sent[way, step, half] = ring_send(
            stage.at[k, :, cols(half)], land.at[way, step, :, cols(half)], sems, way, step, half, z, e
        )

    def add(way, step, half):
        k = (4 - step) if way == 0 else (4 + step) % RING
        sent[way, step - 1, half].wait_recv()
        stage[k, :, cols(half)] = (
            stage[k, :, cols(half)].astype(F32) + land[way, step - 1, :, cols(half)].astype(F32)
        ).astype(BF16)

    if early:
        push(0, 1, 0)
        push(1, 1, 1)
    compute(4)
    push(1, 0, 0)
    push(0, 0, 1)
    if not early:
        compute(3)
        push(0, 1, 0)
        compute(5)
        push(1, 1, 1)
    add(0, 1, 1)
    push(0, 1, 1)
    add(1, 1, 0)
    push(1, 1, 0)
    for step in (2, 3):
        if not early:
            compute(4 - step)
            compute(4 + step)
        for halves in ((0, 1), (1, 0)):
            for way in (0, 1):
                add(way, step, halves[way])
                push(way, step, halves[way])
    if not early:
        compute(0)


def attention_kernel(
    tokens, queries, memory, places, out_weight, gain,
    attended, normed,
    weight, qbuf, kvbuf, posbuf, stage, land, total,
    wsem, lsem, qs, qr, ks, kr, ps, pr, rs, rr,
):
    z, e = lax.axis_index("seq"), lax.axis_index("exp")
    load = pltpu.make_async_copy(out_weight, weight, wsem)
    load.start()
    barrier = pltpu.get_barrier_semaphore()
    peers = exp_peers(e)
    for k in range(1, RING):
        pl.semaphore_signal(barrier, inc=1, device_id=((z + k) % RING, e), device_id_type=MESH)
    for p in peers:
        pl.semaphore_signal(barrier, inc=1, device_id=(z, p), device_id_type=MESH)
    pair = pl.multiple_of(z // 2 * 256, 256)
    local = [
        pltpu.make_async_copy(queries.at[:, pl.ds(pl.multiple_of(z * KEYS, KEYS), KEYS)], qbuf.at[0], lsem.at[0]),
        pltpu.make_async_copy(memory.at[:, pl.ds(pair, 256)], kvbuf.at[31], lsem.at[1]),
        pltpu.make_async_copy(places, posbuf.at[31], lsem.at[2]),
    ]
    for c in local:
        c.start()
    pl.semaphore_wait(barrier, RING - 1 + len(peers))
    queue = {}
    for k in (4, 3, 5, 2, 6, 1, 7):
        to = (z + k) % RING
        queue[RING - k] = pltpu.make_async_remote_copy(
            src_ref=queries.at[:, pl.ds(pl.multiple_of(to * KEYS, KEYS), KEYS)],
            dst_ref=qbuf.at[RING - k],
            send_sem=qs.at[k],
            recv_sem=qr.at[RING - k],
            device_id=(to, e),
            device_id_type=MESH,
        )
        queue[RING - k].start()
    moved = []
    for n, p in enumerate(peers):
        for src, dst, s, r in ((memory.at[:, pl.ds(pair, 256)], kvbuf, ks, kr), (places, posbuf, ps, pr)):
            c = pltpu.make_async_remote_copy(
                src_ref=src, dst_ref=dst.at[n], send_sem=s.at[n], recv_sem=r.at[n],
                device_id=(z, p), device_id_type=MESH,
            )
            c.start()
            moved.append(c)
    for c in local:
        c.wait()
    for c in moved:
        c.wait()
    load.wait()

    def compute(k):
        if k:
            queue[k].wait_recv()
        block = qbuf[k]
        stacked = jnp.concatenate([block[:, h * HD:(h + 1) * HD] for h in range(4)], axis=0)
        key_rows = kvbuf[:, :, 0:HD].reshape(MEM, HD)
        value_rows = kvbuf[:, :, HD:2 * HD].reshape(MEM, HD)
        scores = lax.dot_general(
            key_rows, stacked, (((1,), (1,)), ((), ())), preferred_element_type=F32
        ) * (1.0 / math.sqrt(HD))
        limit = MEM + (z + k) % RING * TOK + lax.broadcasted_iota(jnp.int32, (1, 4 * TOK), 1) % TOK
        where = posbuf[...].reshape(MEM, 128)
        where = jnp.concatenate([where, where], axis=1)
        scores = jnp.where(where <= limit, scores, -1e30)
        top = jnp.max(scores, axis=0, keepdims=True)
        weights = jnp.exp(scores - top)
        probs = (weights / jnp.sum(weights, axis=0, keepdims=True)).astype(BF16)
        context = lax.dot_general(
            probs, value_rows, (((0,), (0,)), ((), ())), preferred_element_type=F32
        ).astype(BF16)
        context = jnp.concatenate([context[h * TOK:(h + 1) * TOK] for h in range(4)], axis=1)

        @pl.loop(0, 4)
        def _(c):
            part = pl.ds(pl.multiple_of(c * 1024, 1024), 1024)
            stage[k, :, part] = jnp.dot(
                context, weight[:, part], preferred_element_type=F32
            ).astype(BF16)

    sent = {}
    reduce_ring(stage, land, (rs, rr), z, e, sent, compute, False)
    square = jnp.zeros((TOK, 1), F32)
    for half in range(2):
        sent[0, 3, half].wait_recv()
        sent[1, 3, half].wait_recv()
        projected = (
            stage[0, :, cols(half)].astype(F32)
            + land[0, 3, :, cols(half)].astype(F32)
            + land[1, 3, :, cols(half)].astype(F32)
        )
        attended[:, cols(half)] = projected.astype(BF16)
        summed = tokens[:, cols(half)].astype(F32) + projected
        total[:, cols(half)] = summed
        square = square + jnp.sum(summed * summed, axis=1, keepdims=True)
    scale = lax.rsqrt(square * (1.0 / D) + 1e-6)
    for half in range(2):
        normed[:, cols(half)] = (total[:, cols(half)] * scale * gain[:, cols(half)]).astype(BF16)
    for c in queue.values():
        c.wait_send()
    for c in sent.values():
        c.wait_send()


def pack(rows, wide, out):
    for c in range(LANES):
        for r in range(CAP):
            wide[pl.ds(c * CAP + r, EXPERTS, stride=PIECE), :] = rows[
                r * EXPERTS:(r + 1) * EXPERTS, c * 128:(c + 1) * 128
            ]
    out[...] = wide[...].astype(BF16)


def unpack(got, wide, out, half):
    wide[...] = got[...].astype(F32)
    for c in range(LANES):
        for r in range(CAP):
            out[r * EXPERTS:(r + 1) * EXPERTS, half * HALF + c * 128:half * HALF + (c + 1) * 128] = wide[
                pl.ds(c * CAP + r, EXPERTS, stride=PIECE), :
            ].astype(BF16)


def expert_kernel(
    normed, pick, mixer, gate, up, down,
    mixture,
    gate_up, low, xs, stage, land, outgo, income, back, home, wide, returned,
    wsem, lsem, as_, ar, bs, br, gs, gr, rs, rr,
):
    z, e = lax.axis_index("seq"), lax.axis_index("exp")
    loads = [
        pltpu.make_async_copy(gate, gate_up.at[0:UNITS], wsem.at[0]),
        pltpu.make_async_copy(up, gate_up.at[UNITS:2 * UNITS], wsem.at[1]),
        pltpu.make_async_copy(down, low, wsem.at[2]),
    ]
    for c in loads:
        c.start()
    barrier = pltpu.get_barrier_semaphore()
    peers = exp_peers(e)
    for k in (1, RING - 1):
        pl.semaphore_signal(barrier, inc=1, device_id=((z + k) % RING, e), device_id_type=MESH)
    for p in peers:
        pl.semaphore_signal(barrier, inc=1, device_id=(z, p), device_id_type=MESH)

    def exchange(src, dst, half, send, recv):
        mine = pl.ds(pl.multiple_of(e * PIECE, 16), PIECE)
        copies = []
        for n, p in enumerate(peers):
            c = pltpu.make_async_remote_copy(
                src_ref=src.at[half, pl.ds(pl.multiple_of(p * PIECE, 16), PIECE)],
                dst_ref=dst.at[half, mine],
                send_sem=send.at[half, n],
                recv_sem=recv.at[half, n],
                device_id=(z, p),
                device_id_type=MESH,
            )
            c.start()
            copies.append(c)
        own = pltpu.make_async_copy(src.at[half, mine], dst.at[half, mine], send.at[half, 31])
        own.start()
        return copies, own

    def picked(half):
        return jnp.dot(pick[...], normed[:, cols(half)], preferred_element_type=F32)

    there, away = {}, {}
    pack(picked(0), wide, outgo.at[0])
    pl.semaphore_wait(barrier, 2 + len(peers))
    there[0] = exchange(outgo, income, 0, as_, ar)
    pack(picked(1), wide, outgo.at[1])
    there[1] = exchange(outgo, income, 1, as_, ar)

    gathered = {}

    def pass_on(way, step, half):
        k = (RING - step) % RING if way == 0 else step
        to = (k + RING - 1) % RING if way == 0 else k + 1
        gathered[way, step, half] = ring_send(
            xs.at[k, :, cols(half)], xs.at[to, :, cols(half)], (gs, gr), way, step, half, z, e
        )

    for half in range(2):
        copies, own = there[half]
        own.wait()
        for c in copies:
            c.wait_recv()
        unpack(income.at[half], wide, xs.at[0], half)
        pass_on(0, 0, half)
        pass_on(1, 0, half)
    for c in loads:
        c.wait()

    def compute(k):
        act = lax.dot_general(
            xs[k], gate_up[...], (((1,), (1,)), ((), ())), preferred_element_type=F32
        )
        gate_act, up_act = act[:, 0:UNITS], act[:, UNITS:2 * UNITS]
        hidden = (gate_act / (1.0 + jnp.exp(-gate_act)) * up_act).astype(BF16)

        @pl.loop(0, 4)
        def _(c):
            part = pl.ds(pl.multiple_of(c * 1024, 1024), 1024)
            stage[k, :, part] = jnp.dot(hidden, low[:, part], preferred_element_type=F32).astype(BF16)

    compute(0)
    for step in (1, 2):
        for half in range(2):
            for way in (0, 1):
                gathered[way, step - 1, half].wait_recv()
                pass_on(way, step, half)
        compute(step)
        compute(RING - step)
    gathered[0, 2, 0].wait_recv()
    pass_on(0, 3, 0)
    gathered[1, 2, 1].wait_recv()
    pass_on(1, 3, 1)
    gathered[0, 2, 1].wait_recv()
    gathered[1, 2, 0].wait_recv()
    compute(3)
    compute(5)

    def last(k):
        gathered[0, 3, 0].wait_recv()
        gathered[1, 3, 1].wait_recv()
        compute(k)

    sent = {}
    reduce_ring(stage, land, (rs, rr), z, e, sent, last, True)
    for half in range(2):
        sent[0, 3, half].wait_recv()
        sent[1, 3, half].wait_recv()
        rows = (
            stage[0, :, cols(half)].astype(F32)
            + land[0, 3, :, cols(half)].astype(F32)
            + land[1, 3, :, cols(half)].astype(F32)
        )
        pack(rows, wide, back.at[half])
        away[half] = exchange(back, home, half, bs, br)
    for half in range(2):
        copies, own = away[half]
        own.wait()
        for c in copies:
            c.wait_recv()
        unpack(home.at[half], wide, returned, half)
        both = jnp.dot(mixer[...], returned[:, cols(half)], preferred_element_type=F32)
        mixture[:, cols(half)] = (both[0:TOK] + both[TOK:2 * TOK]).astype(BF16)
    for half in range(2):
        for c in there[half][0] + away[half][0]:
            c.wait_send()
    for c in list(gathered.values()) + list(sent.values()):
        c.wait_send()


VM = pl.BlockSpec(memory_space=pltpu.VMEM)
HB = pl.BlockSpec(memory_space=pl.ANY)
DMA = pltpu.SemaphoreType.DMA


def body(tokens, queries, memory_kv, memory_pos, out_weight, norm_gain, routes, route_weights, gate_w, up_w, down_w):
    places = jnp.broadcast_to(memory_pos[:, None], (16, 128))
    attended, normed = pl.pallas_call(
        attention_kernel,
        name="attention",
        out_shape=[jax.ShapeDtypeStruct((TOK, D), BF16)] * 2,
        in_specs=[VM, VM, VM, VM, HB, VM],
        out_specs=[VM, VM],
        scratch_shapes=[
            pltpu.VMEM((KEYS, D), BF16),
            pltpu.VMEM((RING, TOK, KEYS), BF16),
            pltpu.VMEM((32, 16, 256), BF16),
            pltpu.VMEM((32, 16, 128), jnp.int32),
            pltpu.VMEM((RING, TOK, D), BF16),
            pltpu.VMEM((2, 4, TOK, D), BF16),
            pltpu.VMEM((TOK, D), F32),
            DMA, DMA((3,)), DMA((RING,)), DMA((RING,)),
            DMA((31,)), DMA((31,)), DMA((31,)), DMA((31,)),
            DMA((2, 4, 2)), DMA((2, 4, 2)),
        ],
        compiler_params=pltpu.CompilerParams(
            collective_id=0, has_side_effects=True, vmem_limit_bytes=40 * 2**20
        ),
    )(
        tokens.reshape(TOK, D), queries.reshape(TOK, D), memory_kv, places, out_weight,
        norm_gain.reshape(1, D),
    )

    names = routes.reshape(TOK, 2)
    one, two = names[:, 0], names[:, 1]
    before = jnp.arange(TOK)[:, None] > jnp.arange(TOK)[None, :]
    rank_one = jnp.sum((one[:, None] == one[None, :]) & before, axis=1, dtype=jnp.int32)
    rank_two = jnp.sum(two[:, None] == one[None, :], axis=1, dtype=jnp.int32) + jnp.sum(
        (two[:, None] == two[None, :]) & before, axis=1, dtype=jnp.int32
    )
    slot_one, slot_two = rank_one * EXPERTS + one, rank_two * EXPERTS + two
    ids = jnp.arange(SLOTS, dtype=jnp.int32)
    pick = ((slot_one[None, :] == ids[:, None]) | (slot_two[None, :] == ids[:, None])).astype(BF16)
    shares = route_weights.reshape(TOK, 2)
    mixer = jnp.where(slot_one[:, None] == ids[None, :], shares[:, 0:1], 0.0) + jnp.where(
        slot_two[:, None] == ids[None, :], shares[:, 1:2], 0.0
    )
    high = mixer.astype(BF16)
    mixer = jnp.concatenate([high, (mixer - high.astype(F32)).astype(BF16)], axis=0)

    mixture = pl.pallas_call(
        expert_kernel,
        name="experts",
        out_shape=jax.ShapeDtypeStruct((TOK, D), BF16),
        in_specs=[VM, VM, VM, HB, HB, HB],
        out_specs=VM,
        scratch_shapes=[
            pltpu.VMEM((2 * UNITS, D), BF16),
            pltpu.VMEM((UNITS, D), BF16),
            pltpu.VMEM((RING, SLOTS, D), BF16),
            pltpu.VMEM((RING, SLOTS, D), BF16),
            pltpu.VMEM((2, 4, SLOTS, D), BF16),
            pltpu.VMEM((2, EXPERTS * PIECE, 128), BF16),
            pltpu.VMEM((2, EXPERTS * PIECE, 128), BF16),
            pltpu.VMEM((2, EXPERTS * PIECE, 128), BF16),
            pltpu.VMEM((2, EXPERTS * PIECE, 128), BF16),
            pltpu.VMEM((EXPERTS * PIECE, 128), F32),
            pltpu.VMEM((SLOTS, D), BF16),
            DMA((3,)), DMA((1,)),
            DMA((2, 32)), DMA((2, 32)), DMA((2, 32)), DMA((2, 32)),
            DMA((2, 4, 2)), DMA((2, 4, 2)), DMA((2, 4, 2)), DMA((2, 4, 2)),
        ],
        compiler_params=pltpu.CompilerParams(
            collective_id=1, has_side_effects=True, vmem_limit_bytes=58 * 2**20
        ),
    )(
        normed, pick, mixer,
        jnp.swapaxes(gate_w[0], 0, 1), jnp.swapaxes(up_w[0], 0, 1), down_w[0],
    )
    return attended.reshape(1, TOK, D), mixture.reshape(1, TOK, D)


def solution(mesh):
    in_specs = (
        P("exp", "seq", None),
        P("exp", "seq", None),
        P("exp", None),
        P("exp"),
        P("seq", None),
        P(),
        P("exp", "seq", None),
        P("exp", "seq", None),
        P("exp", None, "seq"),
        P("exp", None, "seq"),
        P("exp", "seq", None),
    )
    out_specs = (P("exp", "seq", None), P("exp", "seq", None))
    return jax.shard_map(body, mesh=mesh, in_specs=in_specs, out_specs=out_specs, check_vma=False)
```

time: 500 us -> 321 us (0.64)
  waiting for transfers between devices: 327 us -> 0 us
  Pallas kernels: 0 us -> 305 us
  blocking collectives: 74.5 us -> 0 us
  matrix products: 38.5 us -> 0 us
  between operations: 14.6 us -> 0.67 us
  other arithmetic: 16.1 us -> 3.12 us
  local copies, waits for them, and re-layouts: 21.1 us -> 11.4 us
  starting transfers between devices: 7.85 us -> 0 us
    pallas_call x0 -> x2, Pallas kernels: none -> 305 us  [the longest x1 239 us: body(): pl.pallas_call(expert_kernel, name='experts', out_shape=jax.ShapeDtypeStr...]
    reduce_scatter x2 -> x0, waiting for transfers between devices: 162 us -> none  [the longest x1 113 us: body(): lax.psum_scatter(jnp.einsum('nef,efk->nek', rows_part, down_w, preferred_...]
    all_gather x2 -> x0, waiting for transfers between devices: 145 us -> none  [the longest x1 109 us: body(): rows_piece = lax.all_gather(incoming, 'seq', axis=1, tiled=True)]
    all_to_all x2 -> x0, blocking collectives: 60 us -> none  [the longest x1 35.9 us: body(): lax.all_to_all(outgoing, 'exp', split_axis=0, concat_axis=1, tiled=True)]
    dot_general x7 -> x0, matrix products: 38.5 us -> none  [the longest x1 19 us: body(): jnp.einsum('nef,efk->nek', rows_part, down_w, preferred_element_type=jnp....]
    all_to_all x1 -> x0, waiting for transfers between devices: 19.7 us -> none  [body(): lax.all_to_all(returned, 'exp', split_axis=0, concat_axis=1, tiled=True)]
    unnamed x1 -> x0, blocking collectives: 14.4 us -> none
    all_to_all x1 -> x0, other arithmetic: 9.42 us -> none  [body(): lax.all_to_all(returned, 'exp', split_axis=0, concat_axis=1, tiled=True)]
  transfers between devices with their start and end apart: 5 -> 0, of which waited for: 5 -> 0; matrix products, arithmetic and copies ran while one was open for 1% -> 0% of each run, Pallas kernels for 0% -> 0%
where the time goes in v1:
time: 321 us; the launch traced here: 320 us
  Pallas kernels  305 us (95%)
  local copies, waits for them, and re-layouts  11.4 us (4%)
    pallas_call x1, Pallas kernels, body(): pl.pallas_call(expert_kernel, name='experts', out_shape=jax.ShapeDtypeStr...  239 us
    pallas_call x1, Pallas kernels, body(): pl.pallas_call(attention_kernel, name='attention', out_shape=[jax.ShapeDt...  66.3 us
    unnamed x14, local copies, waits for them, and re-layouts  9.19 us

profile of v1, /device:TPU:1, one launch (start us, length us, event | category | flops | bytes accessed | tf_op | source)
XLA Modules:
  0.0 320.1 jit_solution(11540987210231438755)
XLA Ops:
  0.6 0.8 slice_bitcast_fusion.2
  1.4 0.2 convert_reduce_fusion.2
  1.6 0.8 fusion.6
  2.4 0.8 multiply_add_fusion
  3.1 0.8 slice_bitcast_fusion.1
  3.9 0.7 broadcast_in_dim.38.places
  4.6 0.6 fusion.1.pick
  5.2 0.1 fusion.2
  5.4 0.6 pad_maximum_fusion.mixer
  6.0 0.0 copy-start
  6.0 2.2 copy-done
  8.2 0.0 copy-start.2
  8.2 1.0 copy-done.2
  9.2 0.0 copy-start.3
  9.2 1.0 copy-done.3
  10.3 0.0 copy-start.4
  10.3 0.8 copy-done.4
  11.0 0.0 copy-start.5
  11.0 0.7 copy-done.5
  11.7 66.3 %attention.1 = (bf16[64,4096]{1,0:T(8,128)(2,1)S(1)}, bf16[64,4096]{1,0:T(8,128)(2,1)S(1)}) custom-call(bf16[64,4096]{1,0:T(8,128)(2,1)S(1)} %bitcast.39, bf16[64,4096]{1,0:T(8,128)(2,1)S(1)} %bitcast.40, bf16[16,1024]{1,0:T(8,128)(2,1)S(1)} %copy-done.4, s32[16,128]{1,0:T(8,128)S(1)} %broadcast_in_dim.38.places, bf16[512,4096]{1,0:T(8,128)(2,1)S(1)} %copy-done, ...), custom_call_target="tpu_custom_call" | custom-call | tf_op jit(solution)/shard_map/attention/pallas_call | solution.py:362
  78.0 0.0 copy-start.1
  78.0 0.8 copy-done.1
  78.8 238.6 %experts.1 = bf16[64,4096]{1,0:T(8,128)(2,1)} custom-call(bf16[64,4096]{1,0:T(8,128)(2,1)} %copy-done.1, bf16[160,64]{1,0:T(8,128)(2,1)} %fusion.1.pick, bf16[128,160]{1,0:T(8,128)(2,1)} %pad_maximum_fusion.mixer, bf16[192,4096]{1,0:T(8,128)(2,1)} %bitcast.43, bf16[192,4096]{1,0:T(8,128)(2,1)} %bitcast.44, bf16[192,4096]{1,0:T(8,128)(2,1)} %bitcast.45), custom_call_target="tpu_custom_call" | custom-call | tf_op jit(solution)/shard_map/experts/pallas_call | solution.py:405
  317.5 0.8 copy.15
  318.2 1.9 copy.16
Async XLA Ops:
  6.0 2.2 copy-start
  8.2 1.0 copy-start.2
  9.2 1.0 copy-start.3
  10.3 0.8 copy-start.4
  11.0 0.7 copy-start.5
  78.0 0.8 copy-start.1
